TPU v7x, 128 devices: a whole 4x4x4 slice. The times are simulated.
128 devices in a mesh: by: 8 (over y, core), bx: 16 (over z, x).
Axes of the slice: x: 4, y: 4, z: 4, core: 2. Of those that a mesh axis runs over, the one named last changes fastest.
Arguments:
- fields: float32 [3, 8, 2048, 4096], P(None, None, 'by', 'bx'), may hold values from -6 to 6
- level_count: int32 [2048, 4096], P('by', 'bx'), may hold values from 0 to 8, as said below
- thickness: float32 [8], replicated, may hold values from 0.05 to 0.3
- old_pressure: float32 [2048, 4096], P('by', 'bx'), may hold values from -6 to 6
Outputs:
- pressure: float32 [2048, 4096], P('by', 'bx')
- residual: float32 [2048, 4096], P('by', 'bx')
Inputs may be any that keep to these rules, and one draw needn't show every extreme that they name: `level_count`: land comes in aligned squares of 8 x 8 cells, except that the cell at row 1, column 0 is always ocean with all 8 levels.
All inputs are finite; a program needn't handle non-finite values.
Results may differ from a plain program's by a relative error of at most 0.00024.
Values sent between devices are 32-bit elements; how exact they have to be, the bound alone decides.
A program may use at most 128 MiB of HBM per device.

v0:
```python
import jax
import jax.numpy as jnp
from jax import lax
from jax.sharding import Mesh
from jax.sharding import PartitionSpec as P

ITERS = 4
BY_BX = ("by_0", "by_1", "bx_0", "bx_1")
BY = ("by_0", "by_1")
BX = ("bx_0", "bx_1")
VISCOSITY = 0.05
IMPLICIT = 0.05


def padded(array, sides, width):
    for axis, dim in sides:
        size, length = (lax.axis_size(axis), array.shape[dim])
        up = [(i, (i + 1) % size) for i in range(size)]
        down = [(j, i) for i, j in up]
        last = lax.slice_in_dim(array, length - width, length, axis=dim)
        initial = lax.slice_in_dim(array, 0, width, axis=dim)
        before = lax.ppermute(last, axis, up)
        after = lax.ppermute(initial, axis, down)
        array = jnp.concatenate([before, array, after], axis=dim)
    return array


def over_axes(array, axes):
    for axis in axes:
        array = lax.psum(array, axis)
    return array


def laplace(field):
    return (
        field[..., 1:-1, 2:]
        + field[..., 1:-1, :-2]
        + field[..., 2:, 1:-1]
        + field[..., :-2, 1:-1]
        - 4.0 * field[..., 1:-1, 1:-1]
    )


def level_divergence(extended):
    zonal = extended[0]
    meridional = extended[1]
    baroclinic = extended[2]
    tend_zonal = -VISCOSITY * laplace(laplace(zonal)) - 0.5 * (
        baroclinic[..., 2:-2, 3:-1] - baroclinic[..., 2:-2, 1:-3]
    )
    tend_merid = -VISCOSITY * laplace(laplace(meridional)) - 0.5 * (
        baroclinic[..., 3:-1, 2:-2] - baroclinic[..., 1:-3, 2:-2]
    )
    return 0.5 * (tend_zonal[..., 1:-1, 2:] - tend_zonal[..., 1:-1, :-2]) + 0.5 * (
        tend_merid[..., 2:, 1:-1] - tend_merid[..., :-2, 1:-1]
    )


def corner_min(extended_depth):
    return jnp.minimum(
        jnp.minimum(extended_depth[:-1, :-1], extended_depth[:-1, 1:]),
        jnp.minimum(extended_depth[1:, :-1], extended_depth[1:, 1:]),
    )


def operate(extended, corner):
    west_south = extended[:-1, :-1]
    east_south = extended[:-1, 1:]
    west_north = extended[1:, :-1]
    east_north = extended[1:, 1:]
    east_slope = 0.5 * (east_south + east_north - west_south - west_north)
    north_slope = 0.5 * (west_north + east_north - west_south - east_south)
    plus_flux = 0.5 * corner * (east_slope + north_slope)
    minus_flux = 0.5 * corner * (east_slope - north_slope)
    return (
        IMPLICIT * extended[1:-1, 1:-1]
        + plus_flux[:-1, :-1]
        - plus_flux[1:, 1:]
        + minus_flux[1:, :-1]
        - minus_flux[:-1, 1:]
    )


def tile_extend(field):
    return padded(field, ((BY, 0), (BX, 1)), 1)


def paired_dots(residual, precond, image_field):
    return (
        over_axes(jnp.sum(residual * precond), BY_BX),
        over_axes(jnp.sum(precond * image_field), BY_BX),
    )


def solve(right_side, column_depth, first_guess, extend):
    corner = corner_min(extend(column_depth))
    diagonal = IMPLICIT + 0.5 * (
        corner[1:, 1:] + corner[1:, :-1] + corner[:-1, 1:] + corner[:-1, :-1]
    )
    pressure = first_guess
    residual = right_side - operate(extend(pressure), corner)
    precond = residual / diagonal
    image_field = operate(extend(precond), corner)
    norm_now, curvature = paired_dots(residual, precond, image_field)
    step_length = norm_now / curvature
    direction = precond
    image_dir = image_field
    for iteration in range(ITERS):
        pressure = pressure + step_length * direction
        residual = residual - step_length * image_dir
        if iteration + 1 < ITERS:
            precond = residual / diagonal
            image_field = operate(extend(precond), corner)
            norm_next, curvature = paired_dots(residual, precond, image_field)
            ratio_next = norm_next / norm_now
            step_length = norm_next / (curvature - ratio_next * norm_next / step_length)
            direction = precond + ratio_next * direction
            image_dir = image_field + ratio_next * image_dir
            norm_now = norm_next
    return (pressure, residual)


def shards(fields, level_count, thickness, old_pressure):
    levels = jnp.arange(thickness.shape[0], dtype=jnp.int32)[:, None, None]
    wet_mask = (levels < level_count[None]).astype(jnp.float32)
    weights = thickness[:, None, None] * wet_mask
    column_depth = jnp.sum(weights, axis=0)
    extended = padded(fields, ((BY, 2), (BX, 3)), 3)
    forcing_sum = jnp.sum(weights * level_divergence(extended), axis=0)
    ocean_mask = (level_count > 0).astype(jnp.float32)
    right_side = ocean_mask * (forcing_sum + IMPLICIT * old_pressure)
    first_guess = ocean_mask * old_pressure
    pressure, residual = solve(right_side, column_depth, first_guess, tile_extend)
    return (pressure, residual)


def solution(mesh):
    torus = Mesh(mesh.devices.reshape(4, 2, 4, 4), ("by_0", "by_1", "bx_0", "bx_1"))
    in_specs = (P(None, None, BY, BX), P(BY, BX), P(), P(BY, BX))
    out_specs = (P(BY, BX), P(BY, BX))
    return jax.shard_map(
        shards, mesh=torus, in_specs=in_specs, out_specs=out_specs, check_vma=False
    )
```

profile of v0, /device:TPU:0, one launch (start us, length us, event | category | flops | bytes accessed | tf_op | source)
XLA Modules:
  0.0 294.0 jit_solution(12813563485470110456)
XLA Ops:
  7.1 6.8 %copy.16 = f32[3,8,256,256]{2,1,3,0:T(8,128)} copy(f32[3,8,256,256]{3,2,1,0:T(8,128)} %param.4) | data formatting | bytes 12582912 | tf_op args[0]
  21.3 5.0 %collective-permute-start.3 = (f32[3,8,262,3]{2,1,3,0:T(8,128)S(1)}, f32[3,8,262,3]{2,1,3,0:T(8,128)S(1)}, u32[]{:S(2)}, u32[]{:S(2)}) collective-permute-start(f32[3,8,262,3]{2,1,3,0:T(8,128)S(1)} %get-tuple-element.78), channel_id=1, source_target_pairs={{1,0},{2,1},{3,2},{4,3},{5,4},{6,5},{7,6},{8,7},{9,8},{10,9},{11,1... | collective-permute-start | bytes 226376 | tf_op jit(solution)/shard_map/ppermute | solution.py:23
  30.1 6.3 %pad_maximum_fusion = f32[3,8,262,262]{2,1,3,0:T(8,128)} fusion(f32[3,8,262,3]{2,1,3,0:T(8,128)S(1)} %collective-permute-done.3, f32[3,8,3,256]{2,1,3,0:T(8,128)S(1)} %copy-done.1, f32[3,8,256,256]{2,1,3,0:T(8,128)S(1)} %bitcast.7, f32[3,8,3,256]{2,1,3,0:T(8,128)S(1)} %copy-done, f32[3,8,262,3]{2,1,3,0:T(8,128)S(1)} %collective-permute-done.2), kind=kLoop, calls=%fused_computation | loop fusion | flops 6589824 | bytes 13179648 | tf_op jit(solution)/shard_map/concatenate | solution.py:24
  36.4 6.1 %slice_bitcast_fusion.2 = (f32[8,262,262]{1,0,2:T(8,128)S(1)}, f32[8,262,262]{1,0,2:T(8,128)S(1)}, f32[8,262,262]{1,0,2:T(8,128)}) fusion(f32[3,8,262,262]{2,1,3,0:T(8,128)} %pad_maximum_fusion), kind=kLoop, calls=%fused_computation.3 | loop fusion | bytes 13179648 | tf_op jit(solution)/shard_map/squeeze | solution.py:45
  42.5 7.0 %fusion = (f32[8,260,260]{1,0,2:T(8,128)S(1)}, f32[8,260,260]{1,0,2:T(8,128)S(1)}) fusion(f32[8,262,262]{1,0,2:T(8,128)S(1)} %get-tuple-element.80, f32[8,262,262]{1,0,2:T(8,128)S(1)} %get-tuple-element.79), kind=kLoop, calls=%fused_computation.5 | loop fusion | flops 5408000 | bytes 25958400 | tf_op jit(solution)/shard_map/sub | solution.py:36
  49.5 17.4 %fusion.7 = (f32[8,258,258]{1,0,2:T(8,128)}, f32[8,258,258]{1,0,2:T(8,128)}) fusion(f32[8,262,262]{1,0,2:T(8,128)} %get-tuple-element.81, f32[8,260,260]{1,0,2:T(8,128)S(1)} %get-tuple-element.123, f32[8,260,260]{1,0,2:T(8,128)S(1)} %get-tuple-element.122), kind=kLoop, calls=%fused_computation.25 | loop fusion | flops 9585216 | bytes 34080768 | tf_op jit(solution)/shard_map/sub | solution.py:48
  66.9 6.4 %fusion.10 = (f32[256,256]{0,1:T(8,128)S(1)}, f32[256,256]{0,1:T(8,128)S(1)}) fusion(f32[8,258,258]{1,0,2:T(8,128)} %get-tuple-element.85, f32[8,258,258]{1,0,2:T(8,128)} %get-tuple-element.84, f32[8]{0:T(128)S(1)} %copy-done.5, s32[256,256]{0,1:T(8,128)} %copy-done.4), kind=kLoop, calls=%fused_computation.34 | loop fusion | flops 4587520 | bytes 9175072 | tf_op jit(solution)/shard_map/reduce_sum | solution.py:129
  81.6 5.4 %collective-permute-start.7 = (f32[258,1]{0,1:T(1,128)S(1)}, f32[258,1]{0,1:T(1,128)S(1)}, u32[]{:S(2)}, u32[]{:S(2)}) collective-permute-start(f32[258,1]{0,1:T(1,128)S(1)} %get-tuple-element.105), channel_id=1, source_target_pairs={{1,0},{2,1},{3,2},{4,3},{5,4},{6,5},{7,6},{8,7},{9,8},{10,9},{11,1... | collective-permute-start | bytes 3104 | tf_op jit(solution)/shard_map/ppermute | solution.py:23
  102.7 5.6 %collective-permute-done.15 = f32[258,1]{0,1:T(1,128)S(1)} collective-permute-done((f32[258,1]{0,1:T(1,128)S(1)}, f32[258,1]{0,1:T(1,128)S(1)}, u32[]{:S(2)}, u32[]{:S(2)}) %collective-permute-start.15) | collective-permute-done | bytes 1064 | tf_op jit(solution)/shard_map/ppermute | solution.py:22
  109.9 8.3 %all-reduce.11 = (f32[]{:T(128)}, f32[]{:T(128)}) all-reduce(f32[]{:T(128)} %get-tuple-element.13, f32[]{:T(128)} %get-tuple-element.12), channel_id=1, replica_groups=mesh['by_0'=4,'by_1'=2,'bx_0'=4,'bx_1'=4] {'by_0'}, use_global_device_ids=true, to_apply=%region_3.0 | all-reduce | flops 2 | bytes 16 | tf_op jit(solution)/shard_map/psum | solution.py:30
  121.3 8.3 %all-reduce.7 = (f32[]{:T(128)}, f32[]{:T(128)}) all-reduce(f32[]{:T(128)} %get-tuple-element.44, f32[]{:T(128)} %get-tuple-element.45), channel_id=1, replica_groups=mesh['by_0'=4,'by_1'=2,'bx_0'=4,'bx_1'=4] {'bx_0'}, use_global_device_ids=true, to_apply=%region_5.0 | all-reduce | flops 2 | bytes 16 | tf_op jit(solution)/shard_map/psum | solution.py:30
  129.7 8.9 %all-reduce.3 = (f32[]{:T(128)}, f32[]{:T(128)}) all-reduce(f32[]{:T(128)} %get-tuple-element.28, f32[]{:T(128)} %get-tuple-element.29), channel_id=1, replica_groups=mesh['by_0'=4,'by_1'=2,'bx_0'=4,'bx_1'=4] {'bx_1'}, use_global_device_ids=true, to_apply=%region_6.0 | all-reduce | flops 2 | bytes 16 | tf_op jit(solution)/shard_map/psum | solution.py:30
  150.0 5.6 %collective-permute-done.19 = f32[258,1]{0,1:T(1,128)S(1)} collective-permute-done((f32[258,1]{0,1:T(1,128)S(1)}, f32[258,1]{0,1:T(1,128)S(1)}, u32[]{:S(2)}, u32[]{:S(2)}) %collective-permute-start.19) | collective-permute-done | bytes 1064 | tf_op jit(solution)/shard_map/ppermute | solution.py:22
  157.2 9.2 %all-reduce.10 = (f32[]{:T(128)}, f32[]{:T(128)}) all-reduce(f32[]{:T(128)} %get-tuple-element.11, f32[]{:T(128)} %get-tuple-element.10), channel_id=1, replica_groups=mesh['by_0'=4,'by_1'=2,'bx_0'=4,'bx_1'=4] {'by_0'}, use_global_device_ids=true, to_apply=%region_13.0 | all-reduce | flops 2 | bytes 16 | tf_op jit(solution)/shard_map/psum | solution.py:30
  169.5 8.4 %all-reduce.6 = (f32[]{:T(128)}, f32[]{:T(128)}) all-reduce(f32[]{:T(128)} %get-tuple-element.42, f32[]{:T(128)} %get-tuple-element.43), channel_id=1, replica_groups=mesh['by_0'=4,'by_1'=2,'bx_0'=4,'bx_1'=4] {'bx_0'}, use_global_device_ids=true, to_apply=%region_15.0 | all-reduce | flops 2 | bytes 16 | tf_op jit(solution)/shard_map/psum | solution.py:30
  177.9 8.9 %all-reduce.2 = (f32[]{:T(128)}, f32[]{:T(128)}) all-reduce(f32[]{:T(128)} %get-tuple-element.26, f32[]{:T(128)} %get-tuple-element.27), channel_id=1, replica_groups=mesh['by_0'=4,'by_1'=2,'bx_0'=4,'bx_1'=4] {'bx_1'}, use_global_device_ids=true, to_apply=%region_16.0 | all-reduce | flops 2 | bytes 16 | tf_op jit(solution)/shard_map/psum | solution.py:30
  201.4 5.6 %collective-permute-done.23 = f32[258,1]{0,1:T(1,128)S(1)} collective-permute-done((f32[258,1]{0,1:T(1,128)S(1)}, f32[258,1]{0,1:T(1,128)S(1)}, u32[]{:S(2)}, u32[]{:S(2)}) %collective-permute-start.23) | collective-permute-done | bytes 1064 | tf_op jit(solution)/shard_map/ppermute | solution.py:22
  208.6 8.3 %all-reduce.9 = (f32[]{:T(128)}, f32[]{:T(128)}) all-reduce(f32[]{:T(128)} %get-tuple-element.9, f32[]{:T(128)} %get-tuple-element.8), channel_id=1, replica_groups=mesh['by_0'=4,'by_1'=2,'bx_0'=4,'bx_1'=4] {'by_0'}, use_global_device_ids=true, to_apply=%region_23.0 | all-reduce | flops 2 | bytes 16 | tf_op jit(solution)/shard_map/psum | solution.py:30
  220.0 8.3 %all-reduce.5 = (f32[]{:T(128)}, f32[]{:T(128)}) all-reduce(f32[]{:T(128)} %get-tuple-element.40, f32[]{:T(128)} %get-tuple-element.41), channel_id=1, replica_groups=mesh['by_0'=4,'by_1'=2,'bx_0'=4,'bx_1'=4] {'bx_0'}, use_global_device_ids=true, to_apply=%region_25.0 | all-reduce | flops 2 | bytes 16 | tf_op jit(solution)/shard_map/psum | solution.py:30
  228.4 8.9 %all-reduce.1 = (f32[]{:T(128)}, f32[]{:T(128)}) all-reduce(f32[]{:T(128)} %get-tuple-element.24, f32[]{:T(128)} %get-tuple-element.25), channel_id=1, replica_groups=mesh['by_0'=4,'by_1'=2,'bx_0'=4,'bx_1'=4] {'bx_1'}, use_global_device_ids=true, to_apply=%region_26.0 | all-reduce | flops 2 | bytes 16 | tf_op jit(solution)/shard_map/psum | solution.py:30
  251.3 5.6 %collective-permute-done.27 = f32[258,1]{0,1:T(1,128)S(1)} collective-permute-done((f32[258,1]{0,1:T(1,128)S(1)}, f32[258,1]{0,1:T(1,128)S(1)}, u32[]{:S(2)}, u32[]{:S(2)}) %collective-permute-start.27) | collective-permute-done | bytes 1064 | tf_op jit(solution)/shard_map/ppermute | solution.py:22
  258.6 9.2 %all-reduce.8 = (f32[]{:T(128)}, f32[]{:T(128)}) all-reduce(f32[]{:T(128)} %get-tuple-element.7, f32[]{:T(128)} %get-tuple-element.6), channel_id=1, replica_groups=mesh['by_0'=4,'by_1'=2,'bx_0'=4,'bx_1'=4] {'by_0'}, use_global_device_ids=true, to_apply=%region_33.0 | all-reduce | flops 2 | bytes 16 | tf_op jit(solution)/shard_map/psum | solution.py:30
  270.9 8.4 %all-reduce.4 = (f32[]{:T(128)}, f32[]{:T(128)}) all-reduce(f32[]{:T(128)} %get-tuple-element.38, f32[]{:T(128)} %get-tuple-element.39), channel_id=1, replica_groups=mesh['by_0'=4,'by_1'=2,'bx_0'=4,'bx_1'=4] {'bx_0'}, use_global_device_ids=true, to_apply=%region_35.0 | all-reduce | flops 2 | bytes 16 | tf_op jit(solution)/shard_map/psum | solution.py:30
  279.3 9.0 %all-reduce = (f32[]{:T(128)}, f32[]{:T(128)}) all-reduce(f32[]{:T(128)} %get-tuple-element.22, f32[]{:T(128)} %get-tuple-element.23), channel_id=1, replica_groups=mesh['by_0'=4,'by_1'=2,'bx_0'=4,'bx_1'=4] {'bx_1'}, use_global_device_ids=true, to_apply=%region_36.0 | all-reduce | flops 2 | bytes 16 | tf_op jit(solution)/shard_map/psum | solution.py:30
  (120 shorter events, 92.4 us)
Async XLA Ops:
  1.7 12.2 %collective-permute-start = (f32[3,8,3,256]{3,1,2,0:T(8,128)S(1)}, f32[3,8,3,256]{3,1,2,0:T(8,128)S(1)}, u32[]{:S(2)}, u32[]{:S(2)}) collective-permute-start(f32[3,8,3,256]{3,1,2,0:T(8,128)S(1)} %copy.21), channel_id=1, source_target_pairs={{0,16},{16,32},{32,48},{48,64},{64,80},{80,96},{96,112},{112,0},{1... | collective-permute-start | bytes 221192 | tf_op jit(solution)/shard_map/ppermute | solution.py:22
  1.8 14.4 %collective-permute-start.1 = (f32[3,8,3,256]{3,1,2,0:T(8,128)S(1)}, f32[3,8,3,256]{3,1,2,0:T(8,128)S(1)}, u32[]{:S(2)}, u32[]{:S(2)}) collective-permute-start(f32[3,8,3,256]{3,1,2,0:T(8,128)S(1)} %copy.22), channel_id=1, source_target_pairs={{16,0},{32,16},{48,32},{64,48},{80,64},{96,80},{112,96},{0,112},{1... | collective-permute-start | bytes 221192 | tf_op jit(solution)/shard_map/ppermute | solution.py:23
  19.7 10.4 %collective-permute-start.2 = (f32[3,8,262,3]{2,1,3,0:T(8,128)S(1)}, f32[3,8,262,3]{2,1,3,0:T(8,128)S(1)}, u32[]{:S(2)}, u32[]{:S(2)}) collective-permute-start(f32[3,8,262,3]{2,1,3,0:T(8,128)S(1)} %get-tuple-element.77), channel_id=1, source_target_pairs={{0,1},{1,2},{2,3},{3,4},{4,5},{5,6},{6,7},{7,8},{8,9},{9,10},{10,1... | collective-permute-start | bytes 226376 | tf_op jit(solution)/shard_map/ppermute | solution.py:22
  21.3 8.7 %collective-permute-start.3 = (f32[3,8,262,3]{2,1,3,0:T(8,128)S(1)}, f32[3,8,262,3]{2,1,3,0:T(8,128)S(1)}, u32[]{:S(2)}, u32[]{:S(2)}) collective-permute-start(f32[3,8,262,3]{2,1,3,0:T(8,128)S(1)} %get-tuple-element.78), channel_id=1, source_target_pairs={{1,0},{2,1},{3,2},{4,3},{5,4},{6,5},{7,6},{8,7},{9,8},{10,9},{11,1... | collective-permute-start | bytes 226376 | tf_op jit(solution)/shard_map/ppermute | solution.py:23
  27.1 49.3 %collective-permute-start.8 = (f32[1,256]{0,1:T(8,128)}, f32[1,256]{0,1:T(8,128)}, u32[]{:S(2)}, u32[]{:S(2)}) collective-permute-start(f32[1,256]{0,1:T(8,128)} %get-tuple-element.120), channel_id=1, source_target_pairs={{0,16},{16,32},{32,48},{48,64},{64,80},{80,96},{96,112},{112,0},{1... | collective-permute-start | bytes 3080 | tf_op jit(solution)/shard_map/ppermute | solution.py:22
  27.1 49.3 %collective-permute-start.9 = (f32[1,256]{0,1:T(8,128)}, f32[1,256]{0,1:T(8,128)}, u32[]{:S(2)}, u32[]{:S(2)}) collective-permute-start(f32[1,256]{0,1:T(8,128)} %get-tuple-element.121), channel_id=1, source_target_pairs={{16,0},{32,16},{48,32},{64,48},{80,64},{96,80},{112,96},{0,112},{1... | collective-permute-start | bytes 3080 | tf_op jit(solution)/shard_map/ppermute | solution.py:23
  73.4 8.1 %collective-permute-start.4 = (f32[1,256]{0,1:T(8,128)S(1)}, f32[1,256]{0,1:T(8,128)S(1)}, u32[]{:S(2)}, u32[]{:S(2)}) collective-permute-start(f32[1,256]{0,1:T(8,128)S(1)} %get-tuple-element.118), channel_id=1, source_target_pairs={{0,16},{16,32},{32,48},{48,64},{64,80},{80,96},{96,112},{112,0},{1... | collective-permute-start | bytes 3080 | tf_op jit(solution)/shard_map/ppermute | solution.py:22
  73.4 8.1 %collective-permute-start.5 = (f32[1,256]{0,1:T(8,128)S(1)}, f32[1,256]{0,1:T(8,128)S(1)}, u32[]{:S(2)}, u32[]{:S(2)}) collective-permute-start(f32[1,256]{0,1:T(8,128)S(1)} %get-tuple-element.119), channel_id=1, source_target_pairs={{16,0},{32,16},{48,32},{64,48},{80,64},{96,80},{112,96},{0,112},{1... | collective-permute-start | bytes 3080 | tf_op jit(solution)/shard_map/ppermute | solution.py:23
  77.1 9.9 %collective-permute-start.10 = (f32[258,1]{0,1:T(1,128)S(1)}, f32[258,1]{0,1:T(1,128)S(1)}, u32[]{:S(2)}, u32[]{:S(2)}) collective-permute-start(f32[258,1]{0,1:T(1,128)S(1)} %get-tuple-element.109), channel_id=1, source_target_pairs={{1,0},{2,1},{3,2},{4,3},{5,4},{6,5},{7,6},{8,7},{9,8},{10,9},{11,1... | collective-permute-start | bytes 3104 | tf_op jit(solution)/shard_map/ppermute | solution.py:23
  81.5 6.9 %collective-permute-start.11 = (f32[258,1]{0,1:T(1,128)S(1)}, f32[258,1]{0,1:T(1,128)S(1)}, u32[]{:S(2)}, u32[]{:S(2)}) collective-permute-start(f32[258,1]{0,1:T(1,128)S(1)} %get-tuple-element.108), channel_id=1, source_target_pairs={{0,1},{1,2},{2,3},{3,4},{4,5},{5,6},{6,7},{7,8},{8,9},{9,10},{10,1... | collective-permute-start | bytes 3104 | tf_op jit(solution)/shard_map/ppermute | solution.py:22
  81.6 8.3 %collective-permute-start.6 = (f32[258,1]{0,1:T(1,128)S(1)}, f32[258,1]{0,1:T(1,128)S(1)}, u32[]{:S(2)}, u32[]{:S(2)}) collective-permute-start(f32[258,1]{0,1:T(1,128)S(1)} %get-tuple-element.104), channel_id=1, source_target_pairs={{0,1},{1,2},{2,3},{3,4},{4,5},{5,6},{6,7},{7,8},{8,9},{9,10},{10,1... | collective-permute-start | bytes 3104 | tf_op jit(solution)/shard_map/ppermute | solution.py:22
  81.6 8.2 %collective-permute-start.7 = (f32[258,1]{0,1:T(1,128)S(1)}, f32[258,1]{0,1:T(1,128)S(1)}, u32[]{:S(2)}, u32[]{:S(2)}) collective-permute-start(f32[258,1]{0,1:T(1,128)S(1)} %get-tuple-element.105), channel_id=1, source_target_pairs={{1,0},{2,1},{3,2},{4,3},{5,4},{6,5},{7,6},{8,7},{9,8},{10,9},{11,1... | collective-permute-start | bytes 3104 | tf_op jit(solution)/shard_map/ppermute | solution.py:23
  91.7 5.6 %collective-permute-start.12 = (f32[1,256]{0,1:T(8,128)S(1)}, f32[1,256]{0,1:T(8,128)S(1)}, u32[]{:S(2)}, u32[]{:S(2)}) collective-permute-start(f32[1,256]{0,1:T(8,128)S(1)} %get-tuple-element.116), channel_id=1, source_target_pairs={{0,16},{16,32},{32,48},{48,64},{64,80},{80,96},{96,112},{112,0},{1... | collective-permute-start | bytes 3080 | tf_op jit(solution)/shard_map/ppermute | solution.py:22
  91.7 5.6 %collective-permute-start.13 = (f32[1,256]{0,1:T(8,128)S(1)}, f32[1,256]{0,1:T(8,128)S(1)}, u32[]{:S(2)}, u32[]{:S(2)}) collective-permute-start(f32[1,256]{0,1:T(8,128)S(1)} %get-tuple-element.117), channel_id=1, source_target_pairs={{16,0},{32,16},{48,32},{64,48},{80,64},{96,80},{112,96},{0,112},{1... | collective-permute-start | bytes 3080 | tf_op jit(solution)/shard_map/ppermute | solution.py:23
  101.4 6.9 %collective-permute-start.15 = (f32[258,1]{0,1:T(1,128)S(1)}, f32[258,1]{0,1:T(1,128)S(1)}, u32[]{:S(2)}, u32[]{:S(2)}) collective-permute-start(f32[258,1]{0,1:T(1,128)S(1)} %get-tuple-element.100), channel_id=1, source_target_pairs={{0,1},{1,2},{2,3},{3,4},{4,5},{5,6},{6,7},{7,8},{8,9},{9,10},{10,1... | collective-permute-start | bytes 3104 | tf_op jit(solution)/shard_map/ppermute | solution.py:22
  140.1 5.6 %collective-permute-start.16 = (f32[1,256]{0,1:T(8,128)S(1)}, f32[1,256]{0,1:T(8,128)S(1)}, u32[]{:S(2)}, u32[]{:S(2)}) collective-permute-start(f32[1,256]{0,1:T(8,128)S(1)} %get-tuple-element.114), channel_id=1, source_target_pairs={{0,16},{16,32},{32,48},{48,64},{64,80},{80,96},{96,112},{112,0},{1... | collective-permute-start | bytes 3080 | tf_op jit(solution)/shard_map/ppermute | solution.py:22
  140.1 5.6 %collective-permute-start.17 = (f32[1,256]{0,1:T(8,128)S(1)}, f32[1,256]{0,1:T(8,128)S(1)}, u32[]{:S(2)}, u32[]{:S(2)}) collective-permute-start(f32[1,256]{0,1:T(8,128)S(1)} %get-tuple-element.115), channel_id=1, source_target_pairs={{16,0},{32,16},{48,32},{64,48},{80,64},{96,80},{112,96},{0,112},{1... | collective-permute-start | bytes 3080 | tf_op jit(solution)/shard_map/ppermute | solution.py:23
  148.7 6.9 %collective-permute-start.19 = (f32[258,1]{0,1:T(1,128)S(1)}, f32[258,1]{0,1:T(1,128)S(1)}, u32[]{:S(2)}, u32[]{:S(2)}) collective-permute-start(f32[258,1]{0,1:T(1,128)S(1)} %get-tuple-element.96), channel_id=1, source_target_pairs={{0,1},{1,2},{2,3},{3,4},{4,5},{5,6},{6,7},{7,8},{8,9},{9,10},{10,1... | collective-permute-start | bytes 3104 | tf_op jit(solution)/shard_map/ppermute | solution.py:22
  191.5 5.6 %collective-permute-start.20 = (f32[1,256]{0,1:T(8,128)S(1)}, f32[1,256]{0,1:T(8,128)S(1)}, u32[]{:S(2)}, u32[]{:S(2)}) collective-permute-start(f32[1,256]{0,1:T(8,128)S(1)} %get-tuple-element.112), channel_id=1, source_target_pairs={{0,16},{16,32},{32,48},{48,64},{64,80},{80,96},{96,112},{112,0},{1... | collective-permute-start | bytes 3080 | tf_op jit(solution)/shard_map/ppermute | solution.py:22
  191.5 5.6 %collective-permute-start.21 = (f32[1,256]{0,1:T(8,128)S(1)}, f32[1,256]{0,1:T(8,128)S(1)}, u32[]{:S(2)}, u32[]{:S(2)}) collective-permute-start(f32[1,256]{0,1:T(8,128)S(1)} %get-tuple-element.113), channel_id=1, source_target_pairs={{16,0},{32,16},{48,32},{64,48},{80,64},{96,80},{112,96},{0,112},{1... | collective-permute-start | bytes 3080 | tf_op jit(solution)/shard_map/ppermute | solution.py:23
  200.1 6.9 %collective-permute-start.23 = (f32[258,1]{0,1:T(1,128)S(1)}, f32[258,1]{0,1:T(1,128)S(1)}, u32[]{:S(2)}, u32[]{:S(2)}) collective-permute-start(f32[258,1]{0,1:T(1,128)S(1)} %get-tuple-element.92), channel_id=1, source_target_pairs={{0,1},{1,2},{2,3},{3,4},{4,5},{5,6},{6,7},{7,8},{8,9},{9,10},{10,1... | collective-permute-start | bytes 3104 | tf_op jit(solution)/shard_map/ppermute | solution.py:22
  241.4 5.6 %collective-permute-start.24 = (f32[1,256]{0,1:T(8,128)S(1)}, f32[1,256]{0,1:T(8,128)S(1)}, u32[]{:S(2)}, u32[]{:S(2)}) collective-permute-start(f32[1,256]{0,1:T(8,128)S(1)} %get-tuple-element.110), channel_id=1, source_target_pairs={{0,16},{16,32},{32,48},{48,64},{64,80},{80,96},{96,112},{112,0},{1... | collective-permute-start | bytes 3080 | tf_op jit(solution)/shard_map/ppermute | solution.py:22
  241.4 5.6 %collective-permute-start.25 = (f32[1,256]{0,1:T(8,128)S(1)}, f32[1,256]{0,1:T(8,128)S(1)}, u32[]{:S(2)}, u32[]{:S(2)}) collective-permute-start(f32[1,256]{0,1:T(8,128)S(1)} %get-tuple-element.111), channel_id=1, source_target_pairs={{16,0},{32,16},{48,32},{64,48},{80,64},{96,80},{112,96},{0,112},{1... | collective-permute-start | bytes 3080 | tf_op jit(solution)/shard_map/ppermute | solution.py:23
  250.0 6.9 %collective-permute-start.27 = (f32[258,1]{0,1:T(1,128)S(1)}, f32[258,1]{0,1:T(1,128)S(1)}, u32[]{:S(2)}, u32[]{:S(2)}) collective-permute-start(f32[258,1]{0,1:T(1,128)S(1)} %get-tuple-element.88), channel_id=1, source_target_pairs={{0,1},{1,2},{2,3},{3,4},{4,5},{5,6},{6,7},{7,8},{8,9},{9,10},{10,1... | collective-permute-start | bytes 3104 | tf_op jit(solution)/shard_map/ppermute | solution.py:22
  (12 other events, 100.1 us)
where the time goes:
time: 295 us; the launch traced here: 294 us
  blocking collectives  117 us (40%)
  starting transfers between devices  50 us (17%)
  other arithmetic  49.1 us (17%)
  waiting for transfers between devices  39.6 us (13%)
  local copies, waits for them, and re-layouts  24 us (8%)
  between operations  14.7 us (5%)
    psum x16, blocking collectives, over_axes(): array = lax.psum(array, axis)  117 us
    ppermute x14, starting transfers between devices, padded(): after = lax.ppermute(initial, axis, down)  48.2 us
    ppermute x14, waiting for transfers between devices, padded(): before = lax.ppermute(last, axis, up)  34.3 us
    sub x1, other arithmetic, level_divergence(): -VISCOSITY * laplace(laplace(zonal))  17.4 us
    unnamed x23, local copies, waits for them, and re-layouts  11.1 us
    concatenate x12, other arithmetic, padded(): array = jnp.concatenate([before, array, after], axis=dim)  10.6 us
    sub x1, other arithmetic, laplace(): field[..., 1:-1, 2:] + field[..., 1:-1, :-2] + field[..., 2:, 1:-1]  7 us
    reduce_sum x1, other arithmetic, shards(): forcing_sum = jnp.sum(weights * level_divergence(extended), axis=0)  6.36 us
  transfers between devices with their start and end apart: 28, of which 13 were waited for; matrix products, arithmetic and copies ran while one was open for 20% of the time, Pallas kernels for 0%

commit v1 on v0

--- a/solution.py
+++ b/solution.py
@@ -27,7 +27,7 @@
 
 def over_axes(array, axes):
     for axis in axes:
-        array = lax.psum(array, axis)
+        array = jnp.sum(lax.all_gather(array, axis), axis=0)
     return array
 
 

time: 295 us -> 351 us (1.19)
  local copies, waits for them, and re-layouts: 24 us -> 70.3 us
  other arithmetic: 49.1 us -> 68.7 us
  blocking collectives: 117 us -> 106 us
    psum x16 -> x0, blocking collectives: 117 us -> none  [over_axes(): array = lax.psum(array, axis)]
    unnamed x0 -> x16, blocking collectives: none -> 106 us
    unnamed x23 -> x99, local copies, waits for them, and re-layouts: 11.1 us -> 57.5 us
    reduce_sum x0 -> x32, other arithmetic: none -> 19.8 us  [over_axes(): array = jnp.sum(lax.all_gather(array, axis), axis=0)]
  transfers between devices with their start and end apart: 28 -> 28, of which waited for: 13 -> 13; matrix products, arithmetic and copies ran while one was open for 20% -> 17% of each run, Pallas kernels for 0% -> 0%
where the time goes in v1:
time: 351 us; the launch traced here: 349 us
  blocking collectives  106 us (30%)
  local copies, waits for them, and re-layouts  70.3 us (20%)
  other arithmetic  68.7 us (20%)
  starting transfers between devices  50 us (14%)
  waiting for transfers between devices  39 us (11%)
  between operations  14.8 us (4%)
    unnamed x16, blocking collectives  106 us
    unnamed x99, local copies, waits for them, and re-layouts  57.5 us
    ppermute x14, starting transfers between devices, padded(): after = lax.ppermute(initial, axis, down)  48.3 us
    ppermute x14, waiting for transfers between devices, padded(): before = lax.ppermute(last, axis, up)  34.4 us
    reduce_sum x32, other arithmetic, over_axes(): array = jnp.sum(lax.all_gather(array, axis), axis=0)  19.8 us
    sub x1, other arithmetic, level_divergence(): -VISCOSITY * laplace(laplace(zonal))  17.2 us
    concatenate x12, other arithmetic, padded(): array = jnp.concatenate([before, array, after], axis=dim)  10.6 us
  transfers between devices with their start and end apart: 28, of which 13 were waited for; matrix products, arithmetic and copies ran while one was open for 17% of the time, Pallas kernels for 0%

profile of v1, /device:TPU:0, one launch (start us, length us, event | category | flops | bytes accessed | tf_op | source)
XLA Modules:
  0.0 349.2 jit_solution(2437567087362123810)
XLA Ops:
  7.1 6.7 %copy.16 = f32[3,8,256,256]{2,1,3,0:T(8,128)} copy(f32[3,8,256,256]{3,2,1,0:T(8,128)} %param.4) | data formatting | bytes 12582912 | tf_op args[0]
  21.2 5.0 %collective-permute-start.3 = (f32[3,8,262,3]{2,1,3,0:T(8,128)S(1)}, f32[3,8,262,3]{2,1,3,0:T(8,128)S(1)}, u32[]{:S(2)}, u32[]{:S(2)}) collective-permute-start(f32[3,8,262,3]{2,1,3,0:T(8,128)S(1)} %get-tuple-element.78), channel_id=1, source_target_pairs={{1,0},{2,1},{3,2},{4,3},{5,4},{6,5},{7,6},{8,7},{9,8},{10,9},{11,1... | collective-permute-start | bytes 226376 | tf_op jit(solution)/shard_map/ppermute | solution.py:23
  29.9 6.4 %pad_maximum_fusion = f32[3,8,262,262]{2,1,3,0:T(8,128)} fusion(f32[3,8,262,3]{2,1,3,0:T(8,128)S(1)} %collective-permute-done.3, f32[3,8,3,256]{2,1,3,0:T(8,128)S(1)} %copy-done.1, f32[3,8,256,256]{2,1,3,0:T(8,128)S(1)} %bitcast.43, f32[3,8,3,256]{2,1,3,0:T(8,128)S(1)} %copy-done, f32[3,8,262,3]{2,1,3,0:T(8,128)S(1)} %collective-permute-done.2), kind=kLoop, calls=%fused_computation | loop fusion | flops 6589824 | bytes 13179648 | tf_op jit(solution)/shard_map/concatenate | solution.py:24
  36.3 6.1 %slice_bitcast_fusion.2 = (f32[8,262,262]{1,0,2:T(8,128)S(1)}, f32[8,262,262]{1,0,2:T(8,128)S(1)}, f32[8,262,262]{1,0,2:T(8,128)}) fusion(f32[3,8,262,262]{2,1,3,0:T(8,128)} %pad_maximum_fusion), kind=kLoop, calls=%fused_computation.3 | loop fusion | bytes 13179648 | tf_op jit(solution)/shard_map/squeeze | solution.py:45
  42.4 7.0 %fusion = (f32[8,260,260]{1,0,2:T(8,128)S(1)}, f32[8,260,260]{1,0,2:T(8,128)S(1)}) fusion(f32[8,262,262]{1,0,2:T(8,128)S(1)} %get-tuple-element.80, f32[8,262,262]{1,0,2:T(8,128)S(1)} %get-tuple-element.79), kind=kLoop, calls=%fused_computation.5 | loop fusion | flops 5408000 | bytes 25958400 | tf_op jit(solution)/shard_map/sub | solution.py:36
  49.4 17.2 %fusion.7 = (f32[8,258,258]{1,0,2:T(8,128)}, f32[8,258,258]{1,0,2:T(8,128)}) fusion(f32[8,262,262]{1,0,2:T(8,128)} %get-tuple-element.81, f32[8,260,260]{1,0,2:T(8,128)S(1)} %get-tuple-element.123, f32[8,260,260]{1,0,2:T(8,128)S(1)} %get-tuple-element.122), kind=kLoop, calls=%fused_computation.25 | loop fusion | flops 9585216 | bytes 34080768 | tf_op jit(solution)/shard_map/sub | solution.py:48
  66.6 6.3 %fusion.10 = (f32[256,256]{0,1:T(8,128)S(1)}, f32[256,256]{0,1:T(8,128)S(1)}) fusion(f32[8,258,258]{1,0,2:T(8,128)} %get-tuple-element.85, f32[8,258,258]{1,0,2:T(8,128)} %get-tuple-element.84, f32[8]{0:T(128)S(1)} %copy-done.5, s32[256,256]{0,1:T(8,128)} %copy-done.4), kind=kLoop, calls=%fused_computation.34 | loop fusion | flops 4587520 | bytes 9175072 | tf_op jit(solution)/shard_map/reduce_sum | solution.py:129
  81.3 5.4 %collective-permute-start.7 = (f32[258,1]{0,1:T(1,128)S(1)}, f32[258,1]{0,1:T(1,128)S(1)}, u32[]{:S(2)}, u32[]{:S(2)}) collective-permute-start(f32[258,1]{0,1:T(1,128)S(1)} %get-tuple-element.105), channel_id=1, source_target_pairs={{1,0},{2,1},{3,2},{4,3},{5,4},{6,5},{7,6},{8,7},{9,8},{10,9},{11,1... | collective-permute-start | bytes 3104 | tf_op jit(solution)/shard_map/ppermute | solution.py:23
  102.4 5.6 %collective-permute-done.15 = f32[258,1]{0,1:T(1,128)S(1)} collective-permute-done((f32[258,1]{0,1:T(1,128)S(1)}, f32[258,1]{0,1:T(1,128)S(1)}, u32[]{:S(2)}, u32[]{:S(2)}) %collective-permute-start.15) | collective-permute-done | bytes 1064 | tf_op jit(solution)/shard_map/ppermute | solution.py:22
  113.0 7.7 %all-reduce.43 = (f32[4]{0:T(128)S(1)}, f32[4]{0:T(128)S(1)}) all-reduce(f32[4]{0:T(128)S(1)} %dynamic-update-slice, f32[4]{0:T(128)S(1)} %dynamic-update-slice.4), channel_id=1, replica_groups=mesh['by_0'=4,'by_1'=2,'bx_0'=4,'bx_1'=4] {'by_0'}, use_global_device_ids=true, to_apply=%add | all-reduce | flops 8 | bytes 64
  132.5 7.7 %all-reduce.39 = (f32[4]{0:T(128)S(1)}, f32[4]{0:T(128)S(1)}) all-reduce(f32[4]{0:T(128)S(1)} %dynamic-update-slice.2, f32[4]{0:T(128)S(1)} %dynamic-update-slice.6), channel_id=1, replica_groups=mesh['by_0'=4,'by_1'=2,'bx_0'=4,'bx_1'=4] {'bx_0'}, use_global_device_ids=true, to_apply=%add.2 | all-reduce | flops 8 | bytes 64
  144.1 8.3 %all-reduce.35 = (f32[4]{0:T(128)S(1)}, f32[4]{0:T(128)S(1)}) all-reduce(f32[4]{0:T(128)S(1)} %dynamic-update-slice.3, f32[4]{0:T(128)S(1)} %dynamic-update-slice.7), channel_id=1, replica_groups=mesh['by_0'=4,'by_1'=2,'bx_0'=4,'bx_1'=4] {'bx_1'}, use_global_device_ids=true, to_apply=%add.3 | all-reduce | flops 8 | bytes 64
  165.1 5.6 %collective-permute-done.19 = f32[258,1]{0,1:T(1,128)S(1)} collective-permute-done((f32[258,1]{0,1:T(1,128)S(1)}, f32[258,1]{0,1:T(1,128)S(1)}, u32[]{:S(2)}, u32[]{:S(2)}) %collective-permute-start.19) | collective-permute-done | bytes 1064 | tf_op jit(solution)/shard_map/ppermute | solution.py:22
  175.0 8.5 %all-reduce.42 = (f32[4]{0:T(128)S(1)}, f32[4]{0:T(128)S(1)}) all-reduce(f32[4]{0:T(128)S(1)} %dynamic-update-slice.8, f32[4]{0:T(128)S(1)} %dynamic-update-slice.12), channel_id=1, replica_groups=mesh['by_0'=4,'by_1'=2,'bx_0'=4,'bx_1'=4] {'by_0'}, use_global_device_ids=true, to_apply=%add.8 | all-reduce | flops 8 | bytes 64
  194.0 7.9 %all-reduce.38 = (f32[4]{0:T(128)S(1)}, f32[4]{0:T(128)S(1)}) all-reduce(f32[4]{0:T(128)S(1)} %dynamic-update-slice.10, f32[4]{0:T(128)S(1)} %dynamic-update-slice.14), channel_id=1, replica_groups=mesh['by_0'=4,'by_1'=2,'bx_0'=4,'bx_1'=4] {'bx_0'}, use_global_device_ids=true, to_apply=%add.10 | all-reduce | flops 8 | bytes 64
  205.8 8.3 %all-reduce.34 = (f32[4]{0:T(128)S(1)}, f32[4]{0:T(128)S(1)}) all-reduce(f32[4]{0:T(128)S(1)} %dynamic-update-slice.11, f32[4]{0:T(128)S(1)} %dynamic-update-slice.15), channel_id=1, replica_groups=mesh['by_0'=4,'by_1'=2,'bx_0'=4,'bx_1'=4] {'bx_1'}, use_global_device_ids=true, to_apply=%add.11 | all-reduce | flops 8 | bytes 64
  229.8 5.6 %collective-permute-done.23 = f32[258,1]{0,1:T(1,128)S(1)} collective-permute-done((f32[258,1]{0,1:T(1,128)S(1)}, f32[258,1]{0,1:T(1,128)S(1)}, u32[]{:S(2)}, u32[]{:S(2)}) %collective-permute-start.23) | collective-permute-done | bytes 1064 | tf_op jit(solution)/shard_map/ppermute | solution.py:22
  239.9 7.7 %all-reduce.41 = (f32[4]{0:T(128)S(1)}, f32[4]{0:T(128)S(1)}) all-reduce(f32[4]{0:T(128)S(1)} %dynamic-update-slice.16, f32[4]{0:T(128)S(1)} %dynamic-update-slice.20), channel_id=1, replica_groups=mesh['by_0'=4,'by_1'=2,'bx_0'=4,'bx_1'=4] {'by_0'}, use_global_device_ids=true, to_apply=%add.16 | all-reduce | flops 8 | bytes 64
  258.1 7.7 %all-reduce.37 = (f32[4]{0:T(128)S(1)}, f32[4]{0:T(128)S(1)}) all-reduce(f32[4]{0:T(128)S(1)} %dynamic-update-slice.18, f32[4]{0:T(128)S(1)} %dynamic-update-slice.22), channel_id=1, replica_groups=mesh['by_0'=4,'by_1'=2,'bx_0'=4,'bx_1'=4] {'bx_0'}, use_global_device_ids=true, to_apply=%add.18 | all-reduce | flops 8 | bytes 64
  269.7 8.3 %all-reduce.33 = (f32[4]{0:T(128)S(1)}, f32[4]{0:T(128)S(1)}) all-reduce(f32[4]{0:T(128)S(1)} %dynamic-update-slice.19, f32[4]{0:T(128)S(1)} %dynamic-update-slice.23), channel_id=1, replica_groups=mesh['by_0'=4,'by_1'=2,'bx_0'=4,'bx_1'=4] {'bx_1'}, use_global_device_ids=true, to_apply=%add.19 | all-reduce | flops 8 | bytes 64
  293.2 5.6 %collective-permute-done.27 = f32[258,1]{0,1:T(1,128)S(1)} collective-permute-done((f32[258,1]{0,1:T(1,128)S(1)}, f32[258,1]{0,1:T(1,128)S(1)}, u32[]{:S(2)}, u32[]{:S(2)}) %collective-permute-start.27) | collective-permute-done | bytes 1064 | tf_op jit(solution)/shard_map/ppermute | solution.py:22
  303.2 8.5 %all-reduce.40 = (f32[4]{0:T(128)S(1)}, f32[4]{0:T(128)S(1)}) all-reduce(f32[4]{0:T(128)S(1)} %dynamic-update-slice.24, f32[4]{0:T(128)S(1)} %dynamic-update-slice.28), channel_id=1, replica_groups=mesh['by_0'=4,'by_1'=2,'bx_0'=4,'bx_1'=4] {'by_0'}, use_global_device_ids=true, to_apply=%add.24 | all-reduce | flops 8 | bytes 64
  322.3 7.7 %all-reduce.36 = (f32[4]{0:T(128)S(1)}, f32[4]{0:T(128)S(1)}) all-reduce(f32[4]{0:T(128)S(1)} %dynamic-update-slice.26, f32[4]{0:T(128)S(1)} %dynamic-update-slice.30), channel_id=1, replica_groups=mesh['by_0'=4,'by_1'=2,'bx_0'=4,'bx_1'=4] {'bx_0'}, use_global_device_ids=true, to_apply=%add.26 | all-reduce | flops 8 | bytes 64
  333.8 8.3 %all-reduce.32 = (f32[4]{0:T(128)S(1)}, f32[4]{0:T(128)S(1)}) all-reduce(f32[4]{0:T(128)S(1)} %dynamic-update-slice.27, f32[4]{0:T(128)S(1)} %dynamic-update-slice.31), channel_id=1, replica_groups=mesh['by_0'=4,'by_1'=2,'bx_0'=4,'bx_1'=4] {'bx_1'}, use_global_device_ids=true, to_apply=%add.27 | all-reduce | flops 8 | bytes 64
  (228 shorter events, 155.3 us)
Async XLA Ops:
  1.7 12.1 %collective-permute-start = (f32[3,8,3,256]{3,1,2,0:T(8,128)S(1)}, f32[3,8,3,256]{3,1,2,0:T(8,128)S(1)}, u32[]{:S(2)}, u32[]{:S(2)}) collective-permute-start(f32[3,8,3,256]{3,1,2,0:T(8,128)S(1)} %copy.21), channel_id=1, source_target_pairs={{0,16},{16,32},{32,48},{48,64},{64,80},{80,96},{96,112},{112,0},{1... | collective-permute-start | bytes 221192 | tf_op jit(solution)/shard_map/ppermute | solution.py:22
  1.8 14.3 %collective-permute-start.1 = (f32[3,8,3,256]{3,1,2,0:T(8,128)S(1)}, f32[3,8,3,256]{3,1,2,0:T(8,128)S(1)}, u32[]{:S(2)}, u32[]{:S(2)}) collective-permute-start(f32[3,8,3,256]{3,1,2,0:T(8,128)S(1)} %copy.22), channel_id=1, source_target_pairs={{16,0},{32,16},{48,32},{64,48},{80,64},{96,80},{112,96},{0,112},{1... | collective-permute-start | bytes 221192 | tf_op jit(solution)/shard_map/ppermute | solution.py:23
  19.5 10.3 %collective-permute-start.2 = (f32[3,8,262,3]{2,1,3,0:T(8,128)S(1)}, f32[3,8,262,3]{2,1,3,0:T(8,128)S(1)}, u32[]{:S(2)}, u32[]{:S(2)}) collective-permute-start(f32[3,8,262,3]{2,1,3,0:T(8,128)S(1)} %get-tuple-element.77), channel_id=1, source_target_pairs={{0,1},{1,2},{2,3},{3,4},{4,5},{5,6},{6,7},{7,8},{8,9},{9,10},{10,1... | collective-permute-start | bytes 226376 | tf_op jit(solution)/shard_map/ppermute | solution.py:22
  21.2 8.7 %collective-permute-start.3 = (f32[3,8,262,3]{2,1,3,0:T(8,128)S(1)}, f32[3,8,262,3]{2,1,3,0:T(8,128)S(1)}, u32[]{:S(2)}, u32[]{:S(2)}) collective-permute-start(f32[3,8,262,3]{2,1,3,0:T(8,128)S(1)} %get-tuple-element.78), channel_id=1, source_target_pairs={{1,0},{2,1},{3,2},{4,3},{5,4},{6,5},{7,6},{8,7},{9,8},{10,9},{11,1... | collective-permute-start | bytes 226376 | tf_op jit(solution)/shard_map/ppermute | solution.py:23
  26.9 49.1 %collective-permute-start.8 = (f32[1,256]{0,1:T(8,128)}, f32[1,256]{0,1:T(8,128)}, u32[]{:S(2)}, u32[]{:S(2)}) collective-permute-start(f32[1,256]{0,1:T(8,128)} %get-tuple-element.120), channel_id=1, source_target_pairs={{0,16},{16,32},{32,48},{48,64},{64,80},{80,96},{96,112},{112,0},{1... | collective-permute-start | bytes 3080 | tf_op jit(solution)/shard_map/ppermute | solution.py:22
  26.9 49.1 %collective-permute-start.9 = (f32[1,256]{0,1:T(8,128)}, f32[1,256]{0,1:T(8,128)}, u32[]{:S(2)}, u32[]{:S(2)}) collective-permute-start(f32[1,256]{0,1:T(8,128)} %get-tuple-element.121), channel_id=1, source_target_pairs={{16,0},{32,16},{48,32},{64,48},{80,64},{96,80},{112,96},{0,112},{1... | collective-permute-start | bytes 3080 | tf_op jit(solution)/shard_map/ppermute | solution.py:23
  73.0 8.2 %collective-permute-start.4 = (f32[1,256]{0,1:T(8,128)S(1)}, f32[1,256]{0,1:T(8,128)S(1)}, u32[]{:S(2)}, u32[]{:S(2)}) collective-permute-start(f32[1,256]{0,1:T(8,128)S(1)} %get-tuple-element.118), channel_id=1, source_target_pairs={{0,16},{16,32},{32,48},{48,64},{64,80},{80,96},{96,112},{112,0},{1... | collective-permute-start | bytes 3080 | tf_op jit(solution)/shard_map/ppermute | solution.py:22
  73.1 8.1 %collective-permute-start.5 = (f32[1,256]{0,1:T(8,128)S(1)}, f32[1,256]{0,1:T(8,128)S(1)}, u32[]{:S(2)}, u32[]{:S(2)}) collective-permute-start(f32[1,256]{0,1:T(8,128)S(1)} %get-tuple-element.119), channel_id=1, source_target_pairs={{16,0},{32,16},{48,32},{64,48},{80,64},{96,80},{112,96},{0,112},{1... | collective-permute-start | bytes 3080 | tf_op jit(solution)/shard_map/ppermute | solution.py:23
  76.8 9.9 %collective-permute-start.10 = (f32[258,1]{0,1:T(1,128)S(1)}, f32[258,1]{0,1:T(1,128)S(1)}, u32[]{:S(2)}, u32[]{:S(2)}) collective-permute-start(f32[258,1]{0,1:T(1,128)S(1)} %get-tuple-element.109), channel_id=1, source_target_pairs={{1,0},{2,1},{3,2},{4,3},{5,4},{6,5},{7,6},{8,7},{9,8},{10,9},{11,1... | collective-permute-start | bytes 3104 | tf_op jit(solution)/shard_map/ppermute | solution.py:23
  81.2 6.9 %collective-permute-start.11 = (f32[258,1]{0,1:T(1,128)S(1)}, f32[258,1]{0,1:T(1,128)S(1)}, u32[]{:S(2)}, u32[]{:S(2)}) collective-permute-start(f32[258,1]{0,1:T(1,128)S(1)} %get-tuple-element.108), channel_id=1, source_target_pairs={{0,1},{1,2},{2,3},{3,4},{4,5},{5,6},{6,7},{7,8},{8,9},{9,10},{10,1... | collective-permute-start | bytes 3104 | tf_op jit(solution)/shard_map/ppermute | solution.py:22
  81.3 8.3 %collective-permute-start.6 = (f32[258,1]{0,1:T(1,128)S(1)}, f32[258,1]{0,1:T(1,128)S(1)}, u32[]{:S(2)}, u32[]{:S(2)}) collective-permute-start(f32[258,1]{0,1:T(1,128)S(1)} %get-tuple-element.104), channel_id=1, source_target_pairs={{0,1},{1,2},{2,3},{3,4},{4,5},{5,6},{6,7},{7,8},{8,9},{9,10},{10,1... | collective-permute-start | bytes 3104 | tf_op jit(solution)/shard_map/ppermute | solution.py:22
  81.3 8.2 %collective-permute-start.7 = (f32[258,1]{0,1:T(1,128)S(1)}, f32[258,1]{0,1:T(1,128)S(1)}, u32[]{:S(2)}, u32[]{:S(2)}) collective-permute-start(f32[258,1]{0,1:T(1,128)S(1)} %get-tuple-element.105), channel_id=1, source_target_pairs={{1,0},{2,1},{3,2},{4,3},{5,4},{6,5},{7,6},{8,7},{9,8},{10,9},{11,1... | collective-permute-start | bytes 3104 | tf_op jit(solution)/shard_map/ppermute | solution.py:23
  91.4 5.6 %collective-permute-start.12 = (f32[1,256]{0,1:T(8,128)S(1)}, f32[1,256]{0,1:T(8,128)S(1)}, u32[]{:S(2)}, u32[]{:S(2)}) collective-permute-start(f32[1,256]{0,1:T(8,128)S(1)} %get-tuple-element.116), channel_id=1, source_target_pairs={{0,16},{16,32},{32,48},{48,64},{64,80},{80,96},{96,112},{112,0},{1... | collective-permute-start | bytes 3080 | tf_op jit(solution)/shard_map/ppermute | solution.py:22
  91.4 5.6 %collective-permute-start.13 = (f32[1,256]{0,1:T(8,128)S(1)}, f32[1,256]{0,1:T(8,128)S(1)}, u32[]{:S(2)}, u32[]{:S(2)}) collective-permute-start(f32[1,256]{0,1:T(8,128)S(1)} %get-tuple-element.117), channel_id=1, source_target_pairs={{16,0},{32,16},{48,32},{64,48},{80,64},{96,80},{112,96},{0,112},{1... | collective-permute-start | bytes 3080 | tf_op jit(solution)/shard_map/ppermute | solution.py:23
  101.1 6.9 %collective-permute-start.15 = (f32[258,1]{0,1:T(1,128)S(1)}, f32[258,1]{0,1:T(1,128)S(1)}, u32[]{:S(2)}, u32[]{:S(2)}) collective-permute-start(f32[258,1]{0,1:T(1,128)S(1)} %get-tuple-element.100), channel_id=1, source_target_pairs={{0,1},{1,2},{2,3},{3,4},{4,5},{5,6},{6,7},{7,8},{8,9},{9,10},{10,1... | collective-permute-start | bytes 3104 | tf_op jit(solution)/shard_map/ppermute | solution.py:22
  155.1 5.6 %collective-permute-start.16 = (f32[1,256]{0,1:T(8,128)S(1)}, f32[1,256]{0,1:T(8,128)S(1)}, u32[]{:S(2)}, u32[]{:S(2)}) collective-permute-start(f32[1,256]{0,1:T(8,128)S(1)} %get-tuple-element.114), channel_id=1, source_target_pairs={{0,16},{16,32},{32,48},{48,64},{64,80},{80,96},{96,112},{112,0},{1... | collective-permute-start | bytes 3080 | tf_op jit(solution)/shard_map/ppermute | solution.py:22
  155.2 5.6 %collective-permute-start.17 = (f32[1,256]{0,1:T(8,128)S(1)}, f32[1,256]{0,1:T(8,128)S(1)}, u32[]{:S(2)}, u32[]{:S(2)}) collective-permute-start(f32[1,256]{0,1:T(8,128)S(1)} %get-tuple-element.115), channel_id=1, source_target_pairs={{16,0},{32,16},{48,32},{64,48},{80,64},{96,80},{112,96},{0,112},{1... | collective-permute-start | bytes 3080 | tf_op jit(solution)/shard_map/ppermute | solution.py:23
  163.8 6.9 %collective-permute-start.19 = (f32[258,1]{0,1:T(1,128)S(1)}, f32[258,1]{0,1:T(1,128)S(1)}, u32[]{:S(2)}, u32[]{:S(2)}) collective-permute-start(f32[258,1]{0,1:T(1,128)S(1)} %get-tuple-element.96), channel_id=1, source_target_pairs={{0,1},{1,2},{2,3},{3,4},{4,5},{5,6},{6,7},{7,8},{8,9},{9,10},{10,1... | collective-permute-start | bytes 3104 | tf_op jit(solution)/shard_map/ppermute | solution.py:22
  219.9 5.6 %collective-permute-start.20 = (f32[1,256]{0,1:T(8,128)S(1)}, f32[1,256]{0,1:T(8,128)S(1)}, u32[]{:S(2)}, u32[]{:S(2)}) collective-permute-start(f32[1,256]{0,1:T(8,128)S(1)} %get-tuple-element.112), channel_id=1, source_target_pairs={{0,16},{16,32},{32,48},{48,64},{64,80},{80,96},{96,112},{112,0},{1... | collective-permute-start | bytes 3080 | tf_op jit(solution)/shard_map/ppermute | solution.py:22
  219.9 5.6 %collective-permute-start.21 = (f32[1,256]{0,1:T(8,128)S(1)}, f32[1,256]{0,1:T(8,128)S(1)}, u32[]{:S(2)}, u32[]{:S(2)}) collective-permute-start(f32[1,256]{0,1:T(8,128)S(1)} %get-tuple-element.113), channel_id=1, source_target_pairs={{16,0},{32,16},{48,32},{64,48},{80,64},{96,80},{112,96},{0,112},{1... | collective-permute-start | bytes 3080 | tf_op jit(solution)/shard_map/ppermute | solution.py:23
  228.5 6.9 %collective-permute-start.23 = (f32[258,1]{0,1:T(1,128)S(1)}, f32[258,1]{0,1:T(1,128)S(1)}, u32[]{:S(2)}, u32[]{:S(2)}) collective-permute-start(f32[258,1]{0,1:T(1,128)S(1)} %get-tuple-element.92), channel_id=1, source_target_pairs={{0,1},{1,2},{2,3},{3,4},{4,5},{5,6},{6,7},{7,8},{8,9},{9,10},{10,1... | collective-permute-start | bytes 3104 | tf_op jit(solution)/shard_map/ppermute | solution.py:22
  283.3 5.6 %collective-permute-start.24 = (f32[1,256]{0,1:T(8,128)S(1)}, f32[1,256]{0,1:T(8,128)S(1)}, u32[]{:S(2)}, u32[]{:S(2)}) collective-permute-start(f32[1,256]{0,1:T(8,128)S(1)} %get-tuple-element.110), channel_id=1, source_target_pairs={{0,16},{16,32},{32,48},{48,64},{64,80},{80,96},{96,112},{112,0},{1... | collective-permute-start | bytes 3080 | tf_op jit(solution)/shard_map/ppermute | solution.py:22
  283.3 5.6 %collective-permute-start.25 = (f32[1,256]{0,1:T(8,128)S(1)}, f32[1,256]{0,1:T(8,128)S(1)}, u32[]{:S(2)}, u32[]{:S(2)}) collective-permute-start(f32[1,256]{0,1:T(8,128)S(1)} %get-tuple-element.111), channel_id=1, source_target_pairs={{16,0},{32,16},{48,32},{64,48},{80,64},{96,80},{112,96},{0,112},{1... | collective-permute-start | bytes 3080 | tf_op jit(solution)/shard_map/ppermute | solution.py:23
  291.9 6.9 %collective-permute-start.27 = (f32[258,1]{0,1:T(1,128)S(1)}, f32[258,1]{0,1:T(1,128)S(1)}, u32[]{:S(2)}, u32[]{:S(2)}) collective-permute-start(f32[258,1]{0,1:T(1,128)S(1)} %get-tuple-element.88), channel_id=1, source_target_pairs={{0,1},{1,2},{2,3},{3,4},{4,5},{5,6},{6,7},{7,8},{8,9},{9,10},{10,1... | collective-permute-start | bytes 3104 | tf_op jit(solution)/shard_map/ppermute | solution.py:22
  (16 other events, 154.5 us)
